TPU v7x, 256 devices: a whole 4x4x8 slice. The times are simulated.
256 devices in a mesh: sky: 16 (over x, y), freq: 16 (over z, core).
Axes of the slice: x: 4, y: 4, z: 8, core: 2. Of those that a mesh axis runs over, the one named last changes fastest.
Arguments:
- pieces: bfloat16 [128, 128, 128, 128], P('sky', 'freq'), may hold values from -120 to 120
- beam: bfloat16 [128, 128, 128], P('sky'), may hold values from 0.099609375 to 1
- destination: int32 [128], P('sky'), may hold values from 0 to 63, as said below
- clip_tenths: int32 [3, 4], replicated, may hold values from 30 to 60
Outputs:
- significance: float32 [128, 2048, 512], P('freq', 'sky')
Inputs may be any that keep to these rules, and one draw needn't show every extreme that they name: Among the 8 pieces of one index of sky, at most 2 have destinations in one tile, that is with equal destination // 4. In every draw some tile receives exactly 2 pieces from every index of sky.
All inputs are finite; a program needn't handle non-finite values.
Results may differ from a plain program's by a relative error of at most 0.0036.
Values may be sent and summed in bfloat16 or wider, within the bound.
A program may use at most 128 MiB of HBM per device.

v0:
```python
import jax
import jax.numpy as jnp
from jax import lax
from jax.sharding import PartitionSpec as P

ROWB = 1
COLB = 4
RIM = 8
EDGE = 7
KERNELS = 3
REGULARIZER = 0.05
EPSILON = 1e-06
KERNEL_FWHM = (3.0, 6.0, 9.0)
HALF_WIDTHS = (0, 1, 3, 7)


def extended(block, sides, width):
    for axis, dim in sides:
        count = lax.axis_size(axis)
        forward = [(i, i + 1) for i in range(count - 1)]
        backward = [(target, source) for source, target in forward]
        low = lax.ppermute(
            lax.slice_in_dim(block, block.shape[dim] - width, None, axis=dim), axis, forward
        )
        high = lax.ppermute(lax.slice_in_dim(block, 0, width, axis=dim), axis, backward)
        block = jnp.concatenate([low, block, high], axis=dim)
    return block


def kernel_taps(kernel):
    offsets = jnp.arange(-RIM, RIM + 1).astype(jnp.float32)
    sigma = KERNEL_FWHM[kernel] / 2.3548
    return jnp.exp(-offsets * offsets / (2.0 * sigma * sigma)).astype(jnp.bfloat16)


def band_matrix(weights, rows_out, rows_in, shift):
    outer = jnp.arange(rows_out)[:, None]
    inner = jnp.arange(rows_in)[None, :]
    offset = inner - shift - outer
    inside = jnp.abs(offset) <= RIM
    picked = weights[jnp.clip(offset + RIM, 0, 2 * RIM)]
    return jnp.where(inside, picked, jnp.zeros_like(picked))


def smooth(padded, kernel):
    weights = kernel_taps(kernel)
    tall = padded.shape[1] - 2 * RIM
    broad = padded.shape[2]
    across_matrix = band_matrix(weights, broad, broad, 0)
    down_matrix = band_matrix(weights, tall, tall + 2 * RIM, RIM)
    across = jnp.einsum(
        "cyx,zx->cyz", padded, across_matrix, preferred_element_type=jnp.float32
    ).astype(jnp.bfloat16)
    return jnp.einsum(
        "vy,cyz->cvz", down_matrix, across, preferred_element_type=jnp.float32
    ).astype(jnp.bfloat16)


def boxcars(layer):
    channels = layer.shape[0] - 2 * EDGE
    running = layer[EDGE : EDGE + channels].astype(jnp.float32)
    found = [running]
    for step in range(1, EDGE + 1):
        running = (
            running
            + layer[EDGE - step : EDGE - step + channels].astype(jnp.float32)
            + layer[EDGE + step : EDGE + step + channels].astype(jnp.float32)
        )
        if step in HALF_WIDTHS:
            found.append(running)
    return found


def kernel_boxcars(layer):
    found = boxcars(layer)
    power = jnp.stack([jnp.sum(item * item, axis=(1, 2)) for item in found])
    return (found, power)


def raise_score(best, found, totals, thresholds, cells):
    noise_level = jnp.sqrt(totals / cells + EPSILON)
    factor = 10.0 / (thresholds.astype(jnp.float32)[:, None] * noise_level)
    for width, running in enumerate(found):
        best = jnp.maximum(best, jnp.abs(running) * factor[width][:, None, None])
    return best


def owner_tables(beams_in, labels_in, tile_blocks):
    onehot = labels_in[None, :] == jnp.arange(tile_blocks)[:, None]
    beam_wide = beams_in.astype(jnp.float32)
    coverage = (
        jnp.einsum(
            "bs,syx->byx",
            onehot.astype(jnp.float32),
            beam_wide * beam_wide,
            precision=lax.Precision.HIGHEST,
        )
        + REGULARIZER
    )
    return (onehot.astype(jnp.bfloat16), coverage)


def block_values(onehot, coverage, arrived):
    numerator = jnp.einsum("bs,scyx->bcyx", onehot, arrived, preferred_element_type=jnp.float32)
    return (numerator / coverage[:, None]).astype(jnp.bfloat16)


def shards(pieces, beam, destination, clip_tenths):
    sky_count = lax.axis_size("sky")
    piece_count, channels, block_size, _ = pieces.shape
    tile_blocks = ROWB * COLB
    capacity = max(2, 2 * piece_count // sky_count)
    slot_total = sky_count * capacity
    owners = destination // tile_blocks
    numbering = jnp.arange(piece_count)
    earlier = (owners[None, :] == owners[:, None]) & (numbering[None, :] < numbering[:, None])
    position = jnp.sum(earlier.astype(jnp.int32), axis=1)
    slot_index = owners * capacity + position
    weighted = (beam[:, None].astype(jnp.float32) * pieces.astype(jnp.float32)).astype(jnp.bfloat16)
    outgoing = (
        jnp.zeros((slot_total, channels, block_size, block_size), jnp.bfloat16)
        .at[slot_index]
        .set(weighted)
    )
    beams_out = (
        jnp.zeros((slot_total, block_size, block_size), jnp.bfloat16).at[slot_index].set(beam)
    )
    labels_out = (
        jnp.full((slot_total,), -1, jnp.int32).at[slot_index].set(destination % tile_blocks)
    )
    arrived, beams_in, labels_in = (
        lax.all_to_all(outgoing, "sky", split_axis=0, concat_axis=0, tiled=True),
        lax.all_to_all(beams_out, "sky", split_axis=0, concat_axis=0, tiled=True),
        lax.all_to_all(labels_out, "sky", split_axis=0, concat_axis=0, tiled=True),
    )
    onehot, coverage = owner_tables(beams_in, labels_in, tile_blocks)
    tile_values = block_values(onehot, coverage, arrived)
    combined = tile_values.reshape(ROWB, COLB, channels, block_size, block_size).transpose(
        2, 0, 3, 1, 4
    )
    combined = combined.reshape(channels, ROWB * block_size, COLB * block_size)
    padded = extended(combined, (("sky", 1),), RIM)
    smoothed = jnp.stack([smooth(padded, kernel) for kernel in range(KERNELS)])
    planes = extended(smoothed, (("freq", 1),), EDGE)
    cells = float(sky_count * ROWB * block_size * COLB * block_size)
    best = jnp.zeros((channels, ROWB * block_size, COLB * block_size), jnp.float32)
    results = [kernel_boxcars(planes[kernel]) for kernel in range(KERNELS)]
    powers = jnp.stack([item[1] for item in results])
    totals = lax.psum(powers, "sky")
    for kernel in range(KERNELS):
        best = raise_score(best, results[kernel][0], totals[kernel], clip_tenths[kernel], cells)
    return best


def solution(mesh):
    return jax.shard_map(
        shards,
        mesh=mesh,
        in_specs=(P("sky", "freq", None, None), P("sky", None, None), P("sky"), P()),
        out_specs=P("freq", "sky", None),
        check_vma=False,
    )
```

profile of v0, /device:TPU:136, one launch (start us, length us, event | category | flops | bytes accessed | tf_op | source)
XLA Modules:
  0.0 326.6 jit_solution(16188896289594419364)
XLA Ops:
  2.2 7.4 %all-to-all-start = ((s32[16,2,1]{1,2,0:T(1,128)}), s32[16,2,1]{1,2,0:T(1,128)S(1)}, u32[]{:S(2)}, u32[]{:S(2)}) async-start(s32[16,2,1]{1,2,0:T(1,128)} %bitcast), calls=%async_computation | async-start | bytes 16384 | tf_op jit(solution)/shard_map/all_to_all | solution.py:134
  10.8 2.4 scatter_fusion.1
  13.2 2.6 all-to-all-done
  15.8 4.9 %all-to-all-start.2 = ((bf16[32,128,128]{2,1,0:T(8,128)(2,1)}), bf16[32,128,128]{2,1,0:T(8,128)(2,1)S(1)}, u32[]{:S(2)}, u32[]{:S(2)}) async-start(bf16[32,128,128]{2,1,0:T(8,128)(2,1)} %scatter_fusion.1), calls=%async_computation.2 | async-start | bytes 2097152 | tf_op jit(solution)/shard_map/all_to_all | solution.py:133
  20.7 2.2 multiply_convert_fusion
  22.9 5.3 %broadcast_in_dim.12 = bf16[32,8,128,128]{3,2,1,0:T(8,128)(2,1)} broadcast(bf16[]{:T(256)} %constant.32.clone.1), dimensions={} | broadcast | bytes 8388610 | tf_op jit(solution)/shard_map/broadcast_in_dim | solution.py:121
  28.3 5.0 %scatter_fusion = bf16[32,8,128,128]{3,2,1,0:T(8,128)(2,1)} fusion(bf16[32,8,128,128]{3,2,1,0:T(8,128)(2,1)} %broadcast_in_dim.12, s32[8]{0:T(128)S(1)} %compare_select_fusion.2, bf16[8,8,128,128]{3,2,1,0:T(8,128)(2,1)S(1)} %multiply_convert_fusion), kind=kCustom, calls=%fused_computation.1 | custom fusion | bytes 6291488 | tf_op jit(solution)/shard_map/scatter | solution.py:123
  33.3 2.4 all-to-all-done.2
  35.7 5.9 %all-to-all-start.1 = ((bf16[32,8,128,128]{3,2,1,0:T(8,128)(2,1)}), bf16[32,8,128,128]{3,2,1,0:T(8,128)(2,1)}, u32[]{:S(2)}, u32[]{:S(2)}) async-start(bf16[32,8,128,128]{3,2,1,0:T(8,128)(2,1)} %scatter_fusion), calls=%async_computation.1 | async-start | bytes 16777216 | tf_op jit(solution)/shard_map/all_to_all | solution.py:132
  45.4 2.0 fusion.25
  47.3 121.8 %all-to-all-done.1 = bf16[32,8,128,128]{3,2,1,0:T(8,128)(2,1)} async-done(((bf16[32,8,128,128]{3,2,1,0:T(8,128)(2,1)}), bf16[32,8,128,128]{3,2,1,0:T(8,128)(2,1)}, u32[]{:S(2)}, u32[]{:S(2)}) %all-to-all-start.1) | async-done | bytes 8388640 | tf_op jit(solution)/shard_map/all_to_all | solution.py:132
  169.2 8.3 %fusion.54 = bf16[8,1,128,4,128]{4,3,2,0,1:T(4,128)(2,1)S(1)} fusion(f32[4,128,128]{2,0,1:T(4,128)S(1)} %fusion.25, bf16[32,8,128,128]{3,2,1,0:T(8,128)(2,1)} %all-to-all-done.1, s32[32]{0:T(128)S(1)} %eq.33), kind=kOutput, calls=%fused_computation.165 | convolution fusion | flops 34603136 | bytes 9699456 | tf_op jit(solution)/shard_map/bs,scyx->bcyx/dot_general | solution.py:104
  179.9 4.1 %collective-permute-start.1 = (bf16[8,8,512]{2,1,0:T(8,128)(2,1)S(1)}, bf16[8,8,512]{2,1,0:T(8,128)(2,1)S(1)}, u32[]{:S(2)}, u32[]{:S(2)}) collective-permute-start(bf16[8,8,512]{2,1,0:T(8,128)(2,1)S(1)} %get-tuple-element.33), channel_id=1, source_target_pairs={{16,0},{32,16},{48,32},{64,48},{80,64},{96,80},{112,96},{128,112},... | collective-permute-start | bytes 196616 | tf_op jit(solution)/shard_map/ppermute | solution.py:25
  186.0 12.4 %convolution_convert_fusion.4 = bf16[8,512,128]{2,1,0:T(8,128)(2,1)S(1)} fusion(bf16[8,144,512]{2,1,0:T(8,128)(2,1)S(1)} %constant_dynamic-update-slice_fusion, bf16[]{:T(256)} %bitcast.61, bf16[]{:T(256)} %bitcast.62, bf16[]{:T(256)} %bitcast.63, bf16[]{:T(256)} %bitcast.64, bf16[]{:T(256)} %bitcast.65, bf16[]{:T(256)} %bitcast.67, bf16[]{:T(256)} %bitcast.66, ...), kind=kOutput, calls=%fused_computation.93 | convolution fusion | flops 767873024 | bytes 2228834 | tf_op jit(solution)/shard_map/vy,cyz->cvz/dot_general | solution.py:54
  198.4 12.2 %convolution_convert_fusion.5 = bf16[8,512,128]{2,1,0:T(8,128)(2,1)S(1)} fusion(bf16[8,144,512]{2,1,0:T(8,128)(2,1)S(1)} %constant_dynamic-update-slice_fusion, bf16[]{:T(256)} %bitcast.26, bf16[]{:T(256)} %bitcast.27, bf16[]{:T(256)} %bitcast.28, bf16[]{:T(256)} %bitcast.29, bf16[]{:T(256)} %bitcast.30, bf16[]{:T(256)} %bitcast.32, bf16[]{:T(256)} %bitcast.31, ...), kind=kOutput, calls=%fused_computation.94 | convolution fusion | flops 767873024 | bytes 2228834 | tf_op jit(solution)/shard_map/vy,cyz->cvz/dot_general | solution.py:54
  210.6 13.5 %convolution_convert_fusion.3 = bf16[8,512,128]{2,1,0:T(8,128)(2,1)S(1)} fusion(bf16[8,144,512]{2,1,0:T(8,128)(2,1)} %copy-done.6, bf16[]{:T(256)} %bitcast.84, bf16[]{:T(256)} %bitcast.85, bf16[]{:T(256)} %bitcast.86, bf16[]{:T(256)} %bitcast.87, bf16[]{:T(256)} %bitcast.88, bf16[]{:T(256)} %bitcast.90, bf16[]{:T(256)} %bitcast.89, bf16[]{:T(256)} %bitcast.74, ...), kind=kOutput, calls=%fused_computation.92 | convolution fusion | flops 767873024 | bytes 2228834 | tf_op jit(solution)/shard_map/vy,cyz->cvz/dot_general | solution.py:54
  227.7 5.1 %collective-permute-start.3 = (bf16[3,7,128,512]{2,3,1,0:T(8,128)(2,1)S(1)}, bf16[3,7,128,512]{2,3,1,0:T(8,128)(2,1)S(1)}, u32[]{:S(2)}, u32[]{:S(2)}) collective-permute-start(bf16[3,7,128,512]{2,3,1,0:T(8,128)(2,1)S(1)} %get-tuple-element.32), channel_id=1, source_target_pairs={{1,0},{2,1},{3,2},{4,3},{5,4},{6,5},{7,6},{8,7},{9,8},{10,9},{11,1... | collective-permute-start | bytes 8257544 | tf_op jit(solution)/shard_map/ppermute | solution.py:25
  232.8 28.6 %collective-permute-done.2 = bf16[3,7,128,512]{2,3,1,0:T(8,128)(2,1)S(1)} collective-permute-done((bf16[3,7,128,512]{2,3,1,0:T(8,128)(2,1)S(1)}, bf16[3,7,128,512]{2,3,1,0:T(8,128)(2,1)S(1)}, u32[]{:S(2)}, u32[]{:S(2)}) %collective-permute-start.2) | collective-permute-done | bytes 2752544 | tf_op jit(solution)/shard_map/ppermute | solution.py:22
  265.5 3.1 multiply_reduce_fusion.8
  268.6 3.6 %multiply_reduce_fusion.7 = (f32[8]{0:T(128)S(1)}, f32[8,128,512]{1,2,0:T(8,128)S(1)}, f32[8]{0:T(128)S(1)}, f32[8,128,512]{1,2,0:T(8,128)}) fusion(bf16[3,15,128,512]{2,3,1,0:T(8,128)(2,1)S(1)} %get-tuple-element.30, bf16[3,15,128,512]{2,3,1,0:T(8,128)(2,1)S(1)} %get-tuple-element.29, bf16[8,512,128]{2,1,0:T(8,128)(2,1)S(1)} %convolution_convert_fusion.5, ...), kind=kLoop, calls=%fused_computation.85 | loop fusion | flops 17301488 | bytes 22020160 | tf_op jit(solution)/shard_map/reduce_sum | solution.py:76
  272.2 4.1 %multiply_reduce_fusion.6 = (f32[8]{0:T(128)S(1)}, f32[8,128,512]{1,2,0:T(8,128)}, f32[8]{0:T(128)S(1)}, f32[8,128,512]{1,2,0:T(8,128)}) fusion(bf16[3,15,128,512]{2,3,1,0:T(8,128)(2,1)S(1)} %get-tuple-element.30, bf16[3,15,128,512]{2,3,1,0:T(8,128)(2,1)S(1)} %get-tuple-element.29, f32[8,128,512]{1,2,0:T(8,128)S(1)} %get-tuple-element.12, ...), kind=kLoop, calls=%fused_computation.84 | loop fusion | flops 18874352 | bytes 25165888 | tf_op jit(solution)/shard_map/reduce_sum | solution.py:76
  276.4 38.0 %psum.7 = f32[3,4,8]{2,1,0:T(4,128)S(1)} all-reduce(f32[3,4,8]{2,1,0:T(4,128)S(1)} %pad_maximum_fusion.2), channel_id=1, replica_groups=mesh['sky'=16,'freq'=16] {'sky'}, use_global_device_ids=true, to_apply=%region_16.17 | all-reduce | flops 96 | bytes 768 | tf_op jit(solution)/shard_map/psum | solution.py:149
  314.5 9.2 %fusion.14 = f32[8,128,512]{1,2,0:T(8,128)} fusion(f32[8,128,512]{1,2,0:T(8,128)} %get-tuple-element.26, f32[8,128,512]{1,2,0:T(8,128)} %copy-done.2, f32[8,128,512]{1,2,0:T(8,128)} %get-tuple-element.28, f32[8,128,512]{1,2,0:T(8,128)} %copy-done.3, f32[8,128,512]{1,2,0:T(8,128)} %get-tuple-element.14, f32[8,128,512]{1,2,0:T(8,128)} %copy-done.4, ...), kind=kLoop, calls=%fused_computation.31 | loop fusion | flops 26738688 | bytes 24117632 | tf_op jit(solution)/shard_map/max | solution.py:84
  323.7 2.9 copy.18
  (56 shorter events, 19.4 us)
Async XLA Ops:
  0.0 20.7 %copy-start.5 = (bf16[8,128,128]{2,1,0:T(8,128)(2,1)S(1)}, bf16[8,128,128]{2,1,0:T(8,128)(2,1)}, u32[]{:S(2)}) copy-start(bf16[8,128,128]{2,1,0:T(8,128)(2,1)} %param.5) | copy-start | bytes 786436
  2.2 13.6 %all-to-all-start = ((s32[16,2,1]{1,2,0:T(1,128)}), s32[16,2,1]{1,2,0:T(1,128)S(1)}, u32[]{:S(2)}, u32[]{:S(2)}) async-start(s32[16,2,1]{1,2,0:T(1,128)} %bitcast), calls=%async_computation | async-start | bytes 16384 | tf_op jit(solution)/shard_map/all_to_all | solution.py:134
  15.8 19.9 %all-to-all-start.2 = ((bf16[32,128,128]{2,1,0:T(8,128)(2,1)}), bf16[32,128,128]{2,1,0:T(8,128)(2,1)S(1)}, u32[]{:S(2)}, u32[]{:S(2)}) async-start(bf16[32,128,128]{2,1,0:T(8,128)(2,1)} %scatter_fusion.1), calls=%async_computation.2 | async-start | bytes 2097152 | tf_op jit(solution)/shard_map/all_to_all | solution.py:133
  35.7 133.5 %all-to-all-start.1 = ((bf16[32,8,128,128]{3,2,1,0:T(8,128)(2,1)}), bf16[32,8,128,128]{3,2,1,0:T(8,128)(2,1)}, u32[]{:S(2)}, u32[]{:S(2)}) async-start(bf16[32,8,128,128]{3,2,1,0:T(8,128)(2,1)} %scatter_fusion), calls=%async_computation.1 | async-start | bytes 16777216 | tf_op jit(solution)/shard_map/all_to_all | solution.py:132
  177.9 6.2 %collective-permute-start = (bf16[8,8,512]{2,1,0:T(8,128)(2,1)S(1)}, bf16[8,8,512]{2,1,0:T(8,128)(2,1)S(1)}, u32[]{:S(2)}, u32[]{:S(2)}) collective-permute-start(bf16[8,8,512]{2,1,0:T(8,128)(2,1)S(1)} %get-tuple-element.34), channel_id=1, source_target_pairs={{0,16},{16,32},{32,48},{48,64},{64,80},{80,96},{96,112},{112,128},... | collective-permute-start | bytes 196616 | tf_op jit(solution)/shard_map/ppermute | solution.py:22
  179.9 6.2 %collective-permute-start.1 = (bf16[8,8,512]{2,1,0:T(8,128)(2,1)S(1)}, bf16[8,8,512]{2,1,0:T(8,128)(2,1)S(1)}, u32[]{:S(2)}, u32[]{:S(2)}) collective-permute-start(bf16[8,8,512]{2,1,0:T(8,128)(2,1)S(1)} %get-tuple-element.33), channel_id=1, source_target_pairs={{16,0},{32,16},{48,32},{64,48},{80,64},{96,80},{112,96},{128,112},... | collective-permute-start | bytes 196616 | tf_op jit(solution)/shard_map/ppermute | solution.py:25
  186.0 12.4 %copy-start.6 = (bf16[8,144,512]{2,1,0:T(8,128)(2,1)}, bf16[8,144,512]{2,1,0:T(8,128)(2,1)S(1)}, u32[]{:S(2)}) copy-start(bf16[8,144,512]{2,1,0:T(8,128)(2,1)S(1)} %constant_dynamic-update-slice_fusion) | copy-start | bytes 3538948
  224.5 8.3 %copy-start.7 = (s32[3,4]{1,0:T(4,128)S(1)}, s32[3,4]{1,0:T(4,128)}, u32[]{:S(2)}) copy-start(s32[3,4]{1,0:T(4,128)} %param.7) | copy-start | bytes 148
  225.7 35.6 %collective-permute-start.2 = (bf16[3,7,128,512]{2,3,1,0:T(8,128)(2,1)S(1)}, bf16[3,7,128,512]{2,3,1,0:T(8,128)(2,1)S(1)}, u32[]{:S(2)}, u32[]{:S(2)}) collective-permute-start(bf16[3,7,128,512]{2,3,1,0:T(8,128)(2,1)S(1)} %get-tuple-element.31), channel_id=1, source_target_pairs={{0,1},{1,2},{2,3},{3,4},{4,5},{5,6},{6,7},{7,8},{8,9},{9,10},{10,1... | collective-permute-start | bytes 8257544 | tf_op jit(solution)/shard_map/ppermute | solution.py:22
  227.7 35.4 %collective-permute-start.3 = (bf16[3,7,128,512]{2,3,1,0:T(8,128)(2,1)S(1)}, bf16[3,7,128,512]{2,3,1,0:T(8,128)(2,1)S(1)}, u32[]{:S(2)}, u32[]{:S(2)}) collective-permute-start(bf16[3,7,128,512]{2,3,1,0:T(8,128)(2,1)S(1)} %get-tuple-element.32), channel_id=1, source_target_pairs={{1,0},{2,1},{3,2},{4,3},{5,4},{6,5},{7,6},{8,7},{9,8},{10,9},{11,1... | collective-permute-start | bytes 8257544 | tf_op jit(solution)/shard_map/ppermute | solution.py:25
  264.3 8.0 %copy-start = (bf16[3,15,128,512]{2,3,1,0:T(8,128)(2,1)}, bf16[3,15,128,512]{2,3,1,0:T(8,128)(2,1)S(1)}, u32[]{:S(2)}) copy-start(bf16[3,15,128,512]{2,3,1,0:T(8,128)(2,1)S(1)} %get-tuple-element.29) | copy-start | bytes 17694724
  264.3 8.0 %copy-start.1 = (bf16[3,15,128,512]{2,3,1,0:T(8,128)(2,1)}, bf16[3,15,128,512]{2,3,1,0:T(8,128)(2,1)S(1)}, u32[]{:S(2)}) copy-start(bf16[3,15,128,512]{2,3,1,0:T(8,128)(2,1)S(1)} %get-tuple-element.30) | copy-start | bytes 17694724
  265.5 3.1 copy-start.3
  268.6 3.6 %copy-start.2 = (f32[8,128,512]{1,2,0:T(8,128)}, f32[8,128,512]{1,2,0:T(8,128)S(1)}, u32[]{:S(2)}) copy-start(f32[8,128,512]{1,2,0:T(8,128)S(1)} %get-tuple-element.24) | copy-start | bytes 6291460
  272.2 4.2 %copy-start.4 = (f32[8,128,512]{1,2,0:T(8,128)}, f32[8,128,512]{1,2,0:T(8,128)S(1)}, u32[]{:S(2)}) copy-start(f32[8,128,512]{1,2,0:T(8,128)S(1)} %get-tuple-element.12) | copy-start | bytes 6291460
where the time goes:
time: 328 us; the launch traced here: 327 us
  waiting for transfers between devices  159 us (48%)
  matrix products  48.4 us (15%)
  blocking collectives  38 us (12%)
  starting transfers between devices  31.2 us (10%)
  other arithmetic  26.9 us (8%)
  local copies, waits for them, and re-layouts  22.7 us (7%)
    all_to_all x1, waiting for transfers between devices, shards(): lax.all_to_all(outgoing, 'sky', split_axis=0, concat_axis=0, tiled=True)  122 us
    dot_general x3, matrix products, smooth(): jnp.einsum('vy,cyz->cvz', down_matrix, across, preferred_element_type=jnp...  38.1 us
    psum x1, blocking collectives, shards(): totals = lax.psum(powers, 'sky')  38 us
    ppermute x2, waiting for transfers between devices, extended(): lax.ppermute(lax.slice_in_dim(block, block.shape[dim] - width, None, axis...  28.7 us
    reduce_sum x4, other arithmetic, kernel_boxcars(): power = jnp.stack([jnp.sum(item * item, axis=(1, 2)) for item in found])  12 us
    max x1, other arithmetic, raise_score(): best = jnp.maximum(best, jnp.abs(running) * factor[width][:, None, None])  9.23 us
    ppermute x2, starting transfers between devices, extended(): lax.ppermute(lax.slice_in_dim(block, 0, width, axis=dim), axis, backward)  9.17 us
    dot_general x1, matrix products, block_values(): jnp.einsum('bs,scyx->bcyx', onehot, arrived, preferred_element_type=jnp.f...  8.3 us
  transfers between devices with their start and end apart: 7, of which 7 were waited for; matrix products, arithmetic and copies ran while one was open for 7% of the time, Pallas kernels for 0%

commit v1 on v0

--- a/solution.py
+++ b/solution.py
@@ -2,6 +2,7 @@
 import jax.numpy as jnp
 from jax import lax
 from jax.sharding import PartitionSpec as P
+from jax.lax import all_gather
 
 ROWB = 1
 COLB = 4
@@ -146,7 +147,7 @@
     best = jnp.zeros((channels, ROWB * block_size, COLB * block_size), jnp.float32)
     results = [kernel_boxcars(planes[kernel]) for kernel in range(KERNELS)]
     powers = jnp.stack([item[1] for item in results])
-    totals = lax.psum(powers, "sky")
+    totals = all_gather(powers, "sky").sum(axis=0)
     for kernel in range(KERNELS):
         best = raise_score(best, results[kernel][0], totals[kernel], clip_tenths[kernel], cells)
     return best

time: 328 us -> 316 us (0.963)
  blocking collectives: 38 us -> 23.5 us
    psum x1 -> x0, blocking collectives: 38 us -> none  [shards(): totals = lax.psum(powers, 'sky')]
    all_gather x0 -> x1, blocking collectives: none -> 23.5 us  [shards(): totals = all_gather(powers, 'sky').sum(axis=0)]
where the time goes in v1:
time: 316 us; the launch traced here: 312 us
  waiting for transfers between devices  159 us (50%)
  matrix products  48.4 us (15%)
  starting transfers between devices  31.2 us (10%)
  other arithmetic  27 us (9%)
  blocking collectives  23.5 us (7%)
  local copies, waits for them, and re-layouts  22.7 us (7%)
    all_to_all x1, waiting for transfers between devices, shards(): lax.all_to_all(outgoing, 'sky', split_axis=0, concat_axis=0, tiled=True)  122 us
    dot_general x3, matrix products, smooth(): jnp.einsum('vy,cyz->cvz', down_matrix, across, preferred_element_type=jnp...  38.1 us
    ppermute x2, waiting for transfers between devices, extended(): lax.ppermute(lax.slice_in_dim(block, block.shape[dim] - width, None, axis...  28.7 us
    all_gather x1, blocking collectives, shards(): totals = all_gather(powers, 'sky').sum(axis=0)  23.5 us
    reduce_sum x4, other arithmetic, kernel_boxcars(): power = jnp.stack([jnp.sum(item * item, axis=(1, 2)) for item in found])  12 us
    max x1, other arithmetic, raise_score(): best = jnp.maximum(best, jnp.abs(running) * factor[width][:, None, None])  9.23 us
    ppermute x2, starting transfers between devices, extended(): lax.ppermute(lax.slice_in_dim(block, 0, width, axis=dim), axis, backward)  9.17 us
    dot_general x1, matrix products, block_values(): jnp.einsum('bs,scyx->bcyx', onehot, arrived, preferred_element_type=jnp.f...  8.3 us
  transfers between devices with their start and end apart: 7, of which 7 were waited for; matrix products, arithmetic and copies ran while one was open for 7% of the time, Pallas kernels for 0%

profile of v1, /device:TPU:136, one launch (start us, length us, event | category | flops | bytes accessed | tf_op | source)
XLA Modules:
  0.0 312.2 jit_solution(9356636057249901801)
XLA Ops:
  2.2 7.4 %all-to-all-start = ((s32[16,2,1]{1,2,0:T(1,128)}), s32[16,2,1]{1,2,0:T(1,128)S(1)}, u32[]{:S(2)}, u32[]{:S(2)}) async-start(s32[16,2,1]{1,2,0:T(1,128)} %bitcast), calls=%async_computation | async-start | bytes 16384 | tf_op jit(solution)/shard_map/all_to_all | solution.py:135
  10.8 2.4 scatter_fusion.1
  13.2 2.6 all-to-all-done
  15.8 4.9 %all-to-all-start.2 = ((bf16[32,128,128]{2,1,0:T(8,128)(2,1)}), bf16[32,128,128]{2,1,0:T(8,128)(2,1)S(1)}, u32[]{:S(2)}, u32[]{:S(2)}) async-start(bf16[32,128,128]{2,1,0:T(8,128)(2,1)} %scatter_fusion.1), calls=%async_computation.2 | async-start | bytes 2097152 | tf_op jit(solution)/shard_map/all_to_all | solution.py:134
  20.7 2.2 multiply_convert_fusion
  22.9 5.3 %broadcast_in_dim.12 = bf16[32,8,128,128]{3,2,1,0:T(8,128)(2,1)} broadcast(bf16[]{:T(256)} %constant.32.clone.1), dimensions={} | broadcast | bytes 8388610 | tf_op jit(solution)/shard_map/broadcast_in_dim | solution.py:122
  28.3 5.0 %scatter_fusion = bf16[32,8,128,128]{3,2,1,0:T(8,128)(2,1)} fusion(bf16[32,8,128,128]{3,2,1,0:T(8,128)(2,1)} %broadcast_in_dim.12, s32[8]{0:T(128)S(1)} %compare_select_fusion.2, bf16[8,8,128,128]{3,2,1,0:T(8,128)(2,1)S(1)} %multiply_convert_fusion), kind=kCustom, calls=%fused_computation.1 | custom fusion | bytes 6291488 | tf_op jit(solution)/shard_map/scatter | solution.py:124
  33.3 2.4 all-to-all-done.2
  35.7 5.9 %all-to-all-start.1 = ((bf16[32,8,128,128]{3,2,1,0:T(8,128)(2,1)}), bf16[32,8,128,128]{3,2,1,0:T(8,128)(2,1)}, u32[]{:S(2)}, u32[]{:S(2)}) async-start(bf16[32,8,128,128]{3,2,1,0:T(8,128)(2,1)} %scatter_fusion), calls=%async_computation.1 | async-start | bytes 16777216 | tf_op jit(solution)/shard_map/all_to_all | solution.py:133
  45.4 2.0 fusion.25
  47.3 121.8 %all-to-all-done.1 = bf16[32,8,128,128]{3,2,1,0:T(8,128)(2,1)} async-done(((bf16[32,8,128,128]{3,2,1,0:T(8,128)(2,1)}), bf16[32,8,128,128]{3,2,1,0:T(8,128)(2,1)}, u32[]{:S(2)}, u32[]{:S(2)}) %all-to-all-start.1) | async-done | bytes 8388640 | tf_op jit(solution)/shard_map/all_to_all | solution.py:133
  169.2 8.3 %fusion.54 = bf16[8,1,128,4,128]{4,3,2,0,1:T(4,128)(2,1)S(1)} fusion(f32[4,128,128]{2,0,1:T(4,128)S(1)} %fusion.25, bf16[32,8,128,128]{3,2,1,0:T(8,128)(2,1)} %all-to-all-done.1, s32[32]{0:T(128)S(1)} %eq.33), kind=kOutput, calls=%fused_computation.165 | convolution fusion | flops 34603136 | bytes 9699456 | tf_op jit(solution)/shard_map/bs,scyx->bcyx/dot_general | solution.py:105
  179.9 4.1 %collective-permute-start.1 = (bf16[8,8,512]{2,1,0:T(8,128)(2,1)S(1)}, bf16[8,8,512]{2,1,0:T(8,128)(2,1)S(1)}, u32[]{:S(2)}, u32[]{:S(2)}) collective-permute-start(bf16[8,8,512]{2,1,0:T(8,128)(2,1)S(1)} %get-tuple-element.33), channel_id=1, source_target_pairs={{16,0},{32,16},{48,32},{64,48},{80,64},{96,80},{112,96},{128,112},... | collective-permute-start | bytes 196616 | tf_op jit(solution)/shard_map/ppermute | solution.py:26
  186.0 12.4 %convolution_convert_fusion.4 = bf16[8,512,128]{2,1,0:T(8,128)(2,1)S(1)} fusion(bf16[8,144,512]{2,1,0:T(8,128)(2,1)S(1)} %constant_dynamic-update-slice_fusion, bf16[]{:T(256)} %bitcast.61, bf16[]{:T(256)} %bitcast.62, bf16[]{:T(256)} %bitcast.63, bf16[]{:T(256)} %bitcast.64, bf16[]{:T(256)} %bitcast.65, bf16[]{:T(256)} %bitcast.67, bf16[]{:T(256)} %bitcast.66, ...), kind=kOutput, calls=%fused_computation.93 | convolution fusion | flops 767873024 | bytes 2228834 | tf_op jit(solution)/shard_map/vy,cyz->cvz/dot_general | solution.py:55
  198.4 12.2 %convolution_convert_fusion.5 = bf16[8,512,128]{2,1,0:T(8,128)(2,1)S(1)} fusion(bf16[8,144,512]{2,1,0:T(8,128)(2,1)S(1)} %constant_dynamic-update-slice_fusion, bf16[]{:T(256)} %bitcast.26, bf16[]{:T(256)} %bitcast.27, bf16[]{:T(256)} %bitcast.28, bf16[]{:T(256)} %bitcast.29, bf16[]{:T(256)} %bitcast.30, bf16[]{:T(256)} %bitcast.32, bf16[]{:T(256)} %bitcast.31, ...), kind=kOutput, calls=%fused_computation.94 | convolution fusion | flops 767873024 | bytes 2228834 | tf_op jit(solution)/shard_map/vy,cyz->cvz/dot_general | solution.py:55
  210.6 13.5 %convolution_convert_fusion.3 = bf16[8,512,128]{2,1,0:T(8,128)(2,1)S(1)} fusion(bf16[8,144,512]{2,1,0:T(8,128)(2,1)} %copy-done.6, bf16[]{:T(256)} %bitcast.84, bf16[]{:T(256)} %bitcast.85, bf16[]{:T(256)} %bitcast.86, bf16[]{:T(256)} %bitcast.87, bf16[]{:T(256)} %bitcast.88, bf16[]{:T(256)} %bitcast.90, bf16[]{:T(256)} %bitcast.89, bf16[]{:T(256)} %bitcast.74, ...), kind=kOutput, calls=%fused_computation.92 | convolution fusion | flops 767873024 | bytes 2228834 | tf_op jit(solution)/shard_map/vy,cyz->cvz/dot_general | solution.py:55
  227.7 5.1 %collective-permute-start.3 = (bf16[3,7,128,512]{2,3,1,0:T(8,128)(2,1)S(1)}, bf16[3,7,128,512]{2,3,1,0:T(8,128)(2,1)S(1)}, u32[]{:S(2)}, u32[]{:S(2)}) collective-permute-start(bf16[3,7,128,512]{2,3,1,0:T(8,128)(2,1)S(1)} %get-tuple-element.32), channel_id=1, source_target_pairs={{1,0},{2,1},{3,2},{4,3},{5,4},{6,5},{7,6},{8,7},{9,8},{10,9},{11,1... | collective-permute-start | bytes 8257544 | tf_op jit(solution)/shard_map/ppermute | solution.py:26
  232.8 28.6 %collective-permute-done.2 = bf16[3,7,128,512]{2,3,1,0:T(8,128)(2,1)S(1)} collective-permute-done((bf16[3,7,128,512]{2,3,1,0:T(8,128)(2,1)S(1)}, bf16[3,7,128,512]{2,3,1,0:T(8,128)(2,1)S(1)}, u32[]{:S(2)}, u32[]{:S(2)}) %collective-permute-start.2) | collective-permute-done | bytes 2752544 | tf_op jit(solution)/shard_map/ppermute | solution.py:23
  265.5 3.1 multiply_reduce_fusion.8
  268.6 3.6 %multiply_reduce_fusion.7 = (f32[8]{0:T(128)S(1)}, f32[8,128,512]{1,2,0:T(8,128)S(1)}, f32[8]{0:T(128)S(1)}, f32[8,128,512]{1,2,0:T(8,128)}) fusion(bf16[3,15,128,512]{2,3,1,0:T(8,128)(2,1)S(1)} %get-tuple-element.30, bf16[3,15,128,512]{2,3,1,0:T(8,128)(2,1)S(1)} %get-tuple-element.29, bf16[8,512,128]{2,1,0:T(8,128)(2,1)S(1)} %convolution_convert_fusion.5, ...), kind=kLoop, calls=%fused_computation.85 | loop fusion | flops 17301488 | bytes 22020160 | tf_op jit(solution)/shard_map/reduce_sum | solution.py:77
  272.2 4.1 %multiply_reduce_fusion.6 = (f32[8]{0:T(128)S(1)}, f32[8,128,512]{1,2,0:T(8,128)}, f32[8]{0:T(128)S(1)}, f32[8,128,512]{1,2,0:T(8,128)}) fusion(bf16[3,15,128,512]{2,3,1,0:T(8,128)(2,1)S(1)} %get-tuple-element.30, bf16[3,15,128,512]{2,3,1,0:T(8,128)(2,1)S(1)} %get-tuple-element.29, f32[8,128,512]{1,2,0:T(8,128)S(1)} %get-tuple-element.12, ...), kind=kLoop, calls=%fused_computation.84 | loop fusion | flops 18874352 | bytes 25165888 | tf_op jit(solution)/shard_map/reduce_sum | solution.py:77
  276.4 23.5 %all-gather = f32[48,4,8]{2,1,0:T(4,128)S(1)} all-gather(f32[3,4,8]{2,1,0:T(4,128)S(1)} %pad_maximum_fusion.2), channel_id=2, replica_groups=mesh['sky'=16,'freq'=16] {'sky'}, dimensions={0}, use_global_device_ids=true | all-gather | bytes 6528 | tf_op jit(solution)/shard_map/all_gather | solution.py:150
  300.1 9.2 %fusion.14 = f32[8,128,512]{1,2,0:T(8,128)} fusion(f32[8,128,512]{1,2,0:T(8,128)} %get-tuple-element.26, f32[8,128,512]{1,2,0:T(8,128)} %copy-done.2, f32[8,128,512]{1,2,0:T(8,128)} %get-tuple-element.28, f32[8,128,512]{1,2,0:T(8,128)} %copy-done.3, f32[8,128,512]{1,2,0:T(8,128)} %get-tuple-element.14, f32[8,128,512]{1,2,0:T(8,128)} %copy-done.4, ...), kind=kLoop, calls=%fused_computation.31 | loop fusion | flops 26738688 | bytes 24117632 | tf_op jit(solution)/shard_map/max | solution.py:85
  309.3 2.9 copy.18
  (57 shorter events, 19.4 us)
Async XLA Ops:
  0.0 20.7 %copy-start.5 = (bf16[8,128,128]{2,1,0:T(8,128)(2,1)S(1)}, bf16[8,128,128]{2,1,0:T(8,128)(2,1)}, u32[]{:S(2)}) copy-start(bf16[8,128,128]{2,1,0:T(8,128)(2,1)} %param.5) | copy-start | bytes 786436
  2.2 13.6 %all-to-all-start = ((s32[16,2,1]{1,2,0:T(1,128)}), s32[16,2,1]{1,2,0:T(1,128)S(1)}, u32[]{:S(2)}, u32[]{:S(2)}) async-start(s32[16,2,1]{1,2,0:T(1,128)} %bitcast), calls=%async_computation | async-start | bytes 16384 | tf_op jit(solution)/shard_map/all_to_all | solution.py:135
  15.8 19.9 %all-to-all-start.2 = ((bf16[32,128,128]{2,1,0:T(8,128)(2,1)}), bf16[32,128,128]{2,1,0:T(8,128)(2,1)S(1)}, u32[]{:S(2)}, u32[]{:S(2)}) async-start(bf16[32,128,128]{2,1,0:T(8,128)(2,1)} %scatter_fusion.1), calls=%async_computation.2 | async-start | bytes 2097152 | tf_op jit(solution)/shard_map/all_to_all | solution.py:134
  35.7 133.5 %all-to-all-start.1 = ((bf16[32,8,128,128]{3,2,1,0:T(8,128)(2,1)}), bf16[32,8,128,128]{3,2,1,0:T(8,128)(2,1)}, u32[]{:S(2)}, u32[]{:S(2)}) async-start(bf16[32,8,128,128]{3,2,1,0:T(8,128)(2,1)} %scatter_fusion), calls=%async_computation.1 | async-start | bytes 16777216 | tf_op jit(solution)/shard_map/all_to_all | solution.py:133
  177.9 6.2 %collective-permute-start = (bf16[8,8,512]{2,1,0:T(8,128)(2,1)S(1)}, bf16[8,8,512]{2,1,0:T(8,128)(2,1)S(1)}, u32[]{:S(2)}, u32[]{:S(2)}) collective-permute-start(bf16[8,8,512]{2,1,0:T(8,128)(2,1)S(1)} %get-tuple-element.34), channel_id=1, source_target_pairs={{0,16},{16,32},{32,48},{48,64},{64,80},{80,96},{96,112},{112,128},... | collective-permute-start | bytes 196616 | tf_op jit(solution)/shard_map/ppermute | solution.py:23
  179.9 6.2 %collective-permute-start.1 = (bf16[8,8,512]{2,1,0:T(8,128)(2,1)S(1)}, bf16[8,8,512]{2,1,0:T(8,128)(2,1)S(1)}, u32[]{:S(2)}, u32[]{:S(2)}) collective-permute-start(bf16[8,8,512]{2,1,0:T(8,128)(2,1)S(1)} %get-tuple-element.33), channel_id=1, source_target_pairs={{16,0},{32,16},{48,32},{64,48},{80,64},{96,80},{112,96},{128,112},... | collective-permute-start | bytes 196616 | tf_op jit(solution)/shard_map/ppermute | solution.py:26
  186.0 12.4 %copy-start.6 = (bf16[8,144,512]{2,1,0:T(8,128)(2,1)}, bf16[8,144,512]{2,1,0:T(8,128)(2,1)S(1)}, u32[]{:S(2)}) copy-start(bf16[8,144,512]{2,1,0:T(8,128)(2,1)S(1)} %constant_dynamic-update-slice_fusion) | copy-start | bytes 3538948
  224.5 8.3 %copy-start.7 = (s32[3,4]{1,0:T(4,128)S(1)}, s32[3,4]{1,0:T(4,128)}, u32[]{:S(2)}) copy-start(s32[3,4]{1,0:T(4,128)} %param.7) | copy-start | bytes 148
  225.7 35.6 %collective-permute-start.2 = (bf16[3,7,128,512]{2,3,1,0:T(8,128)(2,1)S(1)}, bf16[3,7,128,512]{2,3,1,0:T(8,128)(2,1)S(1)}, u32[]{:S(2)}, u32[]{:S(2)}) collective-permute-start(bf16[3,7,128,512]{2,3,1,0:T(8,128)(2,1)S(1)} %get-tuple-element.31), channel_id=1, source_target_pairs={{0,1},{1,2},{2,3},{3,4},{4,5},{5,6},{6,7},{7,8},{8,9},{9,10},{10,1... | collective-permute-start | bytes 8257544 | tf_op jit(solution)/shard_map/ppermute | solution.py:23
  227.7 35.4 %collective-permute-start.3 = (bf16[3,7,128,512]{2,3,1,0:T(8,128)(2,1)S(1)}, bf16[3,7,128,512]{2,3,1,0:T(8,128)(2,1)S(1)}, u32[]{:S(2)}, u32[]{:S(2)}) collective-permute-start(bf16[3,7,128,512]{2,3,1,0:T(8,128)(2,1)S(1)} %get-tuple-element.32), channel_id=1, source_target_pairs={{1,0},{2,1},{3,2},{4,3},{5,4},{6,5},{7,6},{8,7},{9,8},{10,9},{11,1... | collective-permute-start | bytes 8257544 | tf_op jit(solution)/shard_map/ppermute | solution.py:26
  264.3 8.0 %copy-start = (bf16[3,15,128,512]{2,3,1,0:T(8,128)(2,1)}, bf16[3,15,128,512]{2,3,1,0:T(8,128)(2,1)S(1)}, u32[]{:S(2)}) copy-start(bf16[3,15,128,512]{2,3,1,0:T(8,128)(2,1)S(1)} %get-tuple-element.29) | copy-start | bytes 17694724
  264.3 8.0 %copy-start.1 = (bf16[3,15,128,512]{2,3,1,0:T(8,128)(2,1)}, bf16[3,15,128,512]{2,3,1,0:T(8,128)(2,1)S(1)}, u32[]{:S(2)}) copy-start(bf16[3,15,128,512]{2,3,1,0:T(8,128)(2,1)S(1)} %get-tuple-element.30) | copy-start | bytes 17694724
  265.5 3.1 copy-start.3
  268.6 3.6 %copy-start.2 = (f32[8,128,512]{1,2,0:T(8,128)}, f32[8,128,512]{1,2,0:T(8,128)S(1)}, u32[]{:S(2)}) copy-start(f32[8,128,512]{1,2,0:T(8,128)S(1)} %get-tuple-element.24) | copy-start | bytes 6291460
  272.2 4.2 %copy-start.4 = (f32[8,128,512]{1,2,0:T(8,128)}, f32[8,128,512]{1,2,0:T(8,128)S(1)}, u32[]{:S(2)}) copy-start(f32[8,128,512]{1,2,0:T(8,128)S(1)} %get-tuple-element.12) | copy-start | bytes 6291460
